TPU v7x, 32 devices: a whole 2x2x4 slice. The times are simulated.
32 devices in a mesh: fsdp: 32 (over z, y, x, core).
Axes of the slice: x: 2, y: 2, z: 4, core: 2. Of those that a mesh axis runs over, the one named last changes fastest.
Arguments:
- hidden_in: bfloat16 [32768, 768], P('fsdp'), may hold values from -6 to 6
- lengths: int32 [32], P('fsdp'), may hold values from 512 to 1024, as said below
- ln1_gain: bfloat16 [768], P('fsdp'), may hold values from 0.5 to 1.5
- ln1_bias: bfloat16 [768], P('fsdp'), may hold values from -1.75 to 1.75
- w_qkv: bfloat16 [768, 2304], P('fsdp'), may hold values from -0.3125 to 0.3125
- b_qv: bfloat16 [1536], P('fsdp'), may hold values from -1.75 to 1.75
- w_out: bfloat16 [768, 768], P('fsdp'), may hold values from -0.875 to 0.875
- b_out: bfloat16 [768], P('fsdp'), may hold values from -1.75 to 1.75
- ln2_gain: bfloat16 [768], P('fsdp'), may hold values from 0.5 to 1.5
- ln2_bias: bfloat16 [768], P('fsdp'), may hold values from -1.75 to 1.75
- w_up: bfloat16 [768, 3072], P('fsdp'), may hold values from -0.21875 to 0.21875
- b_up: bfloat16 [3072], P('fsdp'), may hold values from -1.75 to 1.75
- w_down: bfloat16 [3072, 768], P('fsdp'), may hold values from -0.109375 to 0.109375
- b_down: bfloat16 [768], P('fsdp'), may hold values from -1.75 to 1.75
- cotangent: bfloat16 [32768, 768], P('fsdp'), may hold values from -12 to 12
Outputs:
- output: bfloat16 [32768, 768], P('fsdp')
- grad_x: float32 [32768, 768], P('fsdp')
- grad_ln1_gain: float32 [768], P('fsdp')
- grad_ln1_bias: float32 [768], P('fsdp')
- grad_w_qkv: float32 [768, 2304], P('fsdp')
- grad_b_qv: float32 [1536], P('fsdp')
- grad_w_out: float32 [768, 768], P('fsdp')
- grad_b_out: float32 [768], P('fsdp')
- grad_ln2_gain: float32 [768], P('fsdp')
- grad_ln2_bias: float32 [768], P('fsdp')
- grad_w_up: float32 [768, 3072], P('fsdp')
- grad_b_up: float32 [3072], P('fsdp')
- grad_w_down: float32 [3072, 768], P('fsdp')
- grad_b_down: float32 [768], P('fsdp')
Inputs may be any that keep to these rules, and one draw needn't show every extreme that they name: Device d's sequence fills the first lengths[d] of its 1024 slots. In every draw some device holds exactly 1024 tokens and some device exactly 512.
All inputs are finite; a program needn't handle non-finite values.
Results may differ from a plain program's by a relative error of at most 0.012.
The roundings to bfloat16 on the way count: a program that leaves them out, or rounds other values in their place, can miss the bound.
Values may be sent and summed in bfloat16 or wider, within the bound.
A program may use at most 256 MiB of HBM per device.

v0:
```python
import jax
import jax.numpy as jnp
from jax import lax
from jax.sharding import PartitionSpec as P

HEAD_DIM = 64


EPSILON = 1e-05
NEG_FILL = -1e30


def normalize(values, gain_vec, shift_vec):
    row_mean = jnp.mean(values, axis=-1, keepdims=True)
    centred = values - row_mean
    variance = jnp.mean(centred * centred, axis=-1, keepdims=True)
    return centred * lax.rsqrt(variance + EPSILON) * gain_vec + shift_vec


def gelu_tanh(values):
    return jax.nn.gelu(values, approximate=True)


def weight_grad(left, right):
    return lax.dot_general(
        left, right, (((0,), (0,)), ((), ())), preferred_element_type=jnp.float32
    )


def back_product(grad_low, weight):
    return lax.dot_general(
        grad_low, weight, (((1,), (1,)), ((), ())), preferred_element_type=jnp.float32
    )


def allowed_pairs(positions, segment, row_start, row_stop):
    query_pos = positions[row_start:row_stop]
    query_seg = segment[row_start:row_stop]
    same_seg = query_seg[:, None] == segment[None, :row_stop]
    causal = positions[None, :row_stop] <= query_pos[:, None]
    return jnp.logical_and(same_seg, causal)


def block_scores(queries, keys, row_start, row_stop, scale_value):
    products = jnp.einsum(
        "qhd,khd->hqk",
        queries[row_start:row_stop],
        keys[:row_stop],
        preferred_element_type=jnp.float32,
    )
    return products * scale_value


def local(
    hidden_in,
    lengths,
    ln1_gain,
    ln1_bias,
    w_qkv,
    b_qv,
    w_out,
    b_out,
    ln2_gain,
    ln2_bias,
    w_up,
    b_up,
    w_down,
    b_down,
    cotangent,
):
    token_count = hidden_in.shape[0]
    model_width = hidden_in.shape[1]
    head_count = model_width // HEAD_DIM
    scale_value = HEAD_DIM ** (-0.5)
    block_rows = min(512, token_count)
    block_total = token_count // block_rows
    attn_full = (
        lax.all_gather(ln1_gain, "fsdp", axis=0, tiled=True),
        lax.all_gather(ln1_bias, "fsdp", axis=0, tiled=True),
        lax.all_gather(w_qkv, "fsdp", axis=0, tiled=True),
        lax.all_gather(b_qv, "fsdp", axis=0, tiled=True),
        lax.all_gather(w_out, "fsdp", axis=0, tiled=True),
        lax.all_gather(b_out, "fsdp", axis=0, tiled=True),
    )
    mlp_full = (
        lax.all_gather(ln2_gain, "fsdp", axis=0, tiled=True),
        lax.all_gather(ln2_bias, "fsdp", axis=0, tiled=True),
        lax.all_gather(w_up, "fsdp", axis=0, tiled=True),
        lax.all_gather(b_up, "fsdp", axis=0, tiled=True),
        lax.all_gather(w_down, "fsdp", axis=0, tiled=True),
        lax.all_gather(b_down, "fsdp", axis=0, tiled=True),
    )
    gain_one, shift_one, qkv_weight, qv_bias, out_weight, out_bias = attn_full
    gain_two, shift_two, up_weight, up_bias, down_weight, down_bias = mlp_full
    positions = jnp.arange(token_count, dtype=jnp.int32)
    seq_length = lengths[0]
    segment = (positions >= seq_length).astype(jnp.int32)
    live_mask = (positions < seq_length).astype(jnp.float32)[:, None]
    inputs = hidden_in.astype(jnp.float32)
    normed_one = normalize(
        inputs, gain_one.astype(jnp.float32), shift_one.astype(jnp.float32)
    ).astype(jnp.bfloat16)
    bias_full = jnp.concatenate(
        [qv_bias[:model_width], jnp.zeros((model_width,), jnp.bfloat16), qv_bias[model_width:]]
    ).astype(jnp.float32)
    qkv_low = (
        jnp.dot(normed_one, qkv_weight, preferred_element_type=jnp.float32) + bias_full
    ).astype(jnp.bfloat16)
    queries = qkv_low[:, :model_width].reshape(token_count, head_count, HEAD_DIM)
    keys = qkv_low[:, model_width : 2 * model_width].reshape(token_count, head_count, HEAD_DIM)
    values = qkv_low[:, 2 * model_width :].reshape(token_count, head_count, HEAD_DIM)
    attended_parts = []
    lse_parts = []
    for block_index in range(block_total):
        row_start = block_index * block_rows
        row_stop = row_start + block_rows
        allowed = allowed_pairs(positions, segment, row_start, row_stop)
        scores = jnp.where(
            allowed[None], block_scores(queries, keys, row_start, row_stop, scale_value), NEG_FILL
        )
        row_top = jnp.max(scores, axis=-1, keepdims=True)
        exp_scores = jnp.exp(scores - row_top)
        row_total = jnp.sum(exp_scores, axis=-1, keepdims=True)
        probs_low = (exp_scores / row_total).astype(jnp.bfloat16)
        attended_parts.append(
            jnp.einsum(
                "hqk,khd->qhd", probs_low, values[:row_stop], preferred_element_type=jnp.float32
            )
        )
        lse_parts.append(row_top + jnp.log(row_total))
    attended = (
        jnp.concatenate(attended_parts, axis=0)
        .reshape(token_count, model_width)
        .astype(jnp.bfloat16)
    )
    log_totals = jnp.concatenate(lse_parts, axis=1)
    attn_out = jnp.dot(attended, out_weight, preferred_element_type=jnp.float32) + out_bias.astype(
        jnp.float32
    )
    middle = inputs + attn_out
    normed_two = normalize(
        middle, gain_two.astype(jnp.float32), shift_two.astype(jnp.float32)
    ).astype(jnp.bfloat16)
    hidden_pre = jnp.dot(
        normed_two, up_weight, preferred_element_type=jnp.float32
    ) + up_bias.astype(jnp.float32)
    activated = gelu_tanh(hidden_pre).astype(jnp.bfloat16)
    mlp_out = jnp.dot(
        activated, down_weight, preferred_element_type=jnp.float32
    ) + down_bias.astype(jnp.float32)
    output = (live_mask * (middle + mlp_out)).astype(jnp.bfloat16)
    back_gain_two, back_shift_two, back_up, back_down = (
        lax.all_gather(ln2_gain, "fsdp", axis=0, tiled=True),
        lax.all_gather(ln2_bias, "fsdp", axis=0, tiled=True),
        lax.all_gather(w_up, "fsdp", axis=0, tiled=True),
        lax.all_gather(w_down, "fsdp", axis=0, tiled=True),
    )
    back_gain_one, back_shift_one, back_qkv, back_out = (
        lax.all_gather(ln1_gain, "fsdp", axis=0, tiled=True),
        lax.all_gather(ln1_bias, "fsdp", axis=0, tiled=True),
        lax.all_gather(w_qkv, "fsdp", axis=0, tiled=True),
        lax.all_gather(w_out, "fsdp", axis=0, tiled=True),
    )
    grad_out = cotangent.astype(jnp.float32) * live_mask
    grad_out_low = grad_out.astype(jnp.bfloat16)
    grad_w_down = weight_grad(activated, grad_out_low)
    grad_b_down = jnp.sum(grad_out, axis=0)
    grad_act = back_product(grad_out_low, back_down)
    gelu_back = jax.vjp(gelu_tanh, hidden_pre)[1]
    grad_hidden = gelu_back(grad_act)[0].astype(jnp.bfloat16)
    normed_again, norm_two_back = jax.vjp(
        normalize, middle, back_gain_two.astype(jnp.float32), back_shift_two.astype(jnp.float32)
    )
    grad_w_up = weight_grad(normed_again.astype(jnp.bfloat16), grad_hidden)
    grad_b_up = jnp.sum(grad_hidden.astype(jnp.float32), axis=0)
    grad_middle_norm, grad_ln2_gain, grad_ln2_bias = norm_two_back(
        back_product(grad_hidden, back_up)
    )
    grad_middle = grad_out + grad_middle_norm
    grad_attn_low = grad_middle.astype(jnp.bfloat16)
    grad_w_out = weight_grad(attended, grad_attn_low)
    grad_b_out = jnp.sum(grad_attn_low.astype(jnp.float32), axis=0)
    grad_attended = (
        back_product(grad_attn_low, back_out)
        .astype(jnp.bfloat16)
        .reshape(token_count, head_count, HEAD_DIM)
    )
    query_parts = []
    grad_keys = jnp.zeros((token_count, head_count, HEAD_DIM), jnp.float32)
    grad_values = jnp.zeros((token_count, head_count, HEAD_DIM), jnp.float32)
    for block_index in range(block_total):
        row_start = block_index * block_rows
        row_stop = row_start + block_rows
        allowed = allowed_pairs(positions, segment, row_start, row_stop)
        scores = jnp.where(
            allowed[None], block_scores(queries, keys, row_start, row_stop, scale_value), NEG_FILL
        )
        probs_back = jnp.where(
            allowed[None], jnp.exp(scores - log_totals[:, row_start:row_stop]), 0.0
        )
        grad_block = grad_attended[row_start:row_stop]
        grad_probs = jnp.einsum(
            "qhd,khd->hqk", grad_block, values[:row_stop], preferred_element_type=jnp.float32
        )
        row_delta = jnp.sum(probs_back * grad_probs, axis=-1, keepdims=True)
        grad_scores = (probs_back * (grad_probs - row_delta)).astype(jnp.bfloat16)
        query_parts.append(
            scale_value
            * jnp.einsum(
                "hqk,khd->qhd", grad_scores, keys[:row_stop], preferred_element_type=jnp.float32
            )
        )
        grad_keys = grad_keys.at[:row_stop].add(
            scale_value
            * jnp.einsum(
                "hqk,qhd->khd",
                grad_scores,
                queries[row_start:row_stop],
                preferred_element_type=jnp.float32,
            )
        )
        grad_values = grad_values.at[:row_stop].add(
            jnp.einsum(
                "hqk,qhd->khd",
                probs_back.astype(jnp.bfloat16),
                grad_block,
                preferred_element_type=jnp.float32,
            )
        )
    grad_queries = jnp.concatenate(query_parts, axis=0)
    grad_qkv = jnp.concatenate(
        [
            grad_queries.reshape(token_count, model_width).astype(jnp.bfloat16),
            grad_keys.reshape(token_count, model_width).astype(jnp.bfloat16),
            grad_values.reshape(token_count, model_width).astype(jnp.bfloat16),
        ],
        axis=1,
    )
    normed_first, norm_one_back = jax.vjp(
        normalize, inputs, back_gain_one.astype(jnp.float32), back_shift_one.astype(jnp.float32)
    )
    grad_w_qkv = weight_grad(normed_first.astype(jnp.bfloat16), grad_qkv)
    grad_b_qv = jnp.concatenate(
        [
            jnp.sum(grad_qkv[:, :model_width].astype(jnp.float32), axis=0),
            jnp.sum(grad_qkv[:, 2 * model_width :].astype(jnp.float32), axis=0),
        ]
    )
    grad_in_norm, grad_ln1_gain, grad_ln1_bias = norm_one_back(back_product(grad_qkv, back_qkv))
    grad_inputs = grad_middle + grad_in_norm
    shards = (
        lax.psum_scatter(grad_ln1_gain, "fsdp", scatter_dimension=0, tiled=True),
        lax.psum_scatter(grad_ln1_bias, "fsdp", scatter_dimension=0, tiled=True),
        lax.psum_scatter(grad_w_qkv, "fsdp", scatter_dimension=0, tiled=True),
        lax.psum_scatter(grad_b_qv, "fsdp", scatter_dimension=0, tiled=True),
        lax.psum_scatter(grad_w_out, "fsdp", scatter_dimension=0, tiled=True),
        lax.psum_scatter(grad_b_out, "fsdp", scatter_dimension=0, tiled=True),
        lax.psum_scatter(grad_ln2_gain, "fsdp", scatter_dimension=0, tiled=True),
        lax.psum_scatter(grad_ln2_bias, "fsdp", scatter_dimension=0, tiled=True),
        lax.psum_scatter(grad_w_up, "fsdp", scatter_dimension=0, tiled=True),
        lax.psum_scatter(grad_b_up, "fsdp", scatter_dimension=0, tiled=True),
        lax.psum_scatter(grad_w_down, "fsdp", scatter_dimension=0, tiled=True),
        lax.psum_scatter(grad_b_down, "fsdp", scatter_dimension=0, tiled=True),
    )
    return (
        output,
        grad_inputs,
        shards[0],
        shards[1],
        shards[2],
        shards[3],
        shards[4],
        shards[5],
        shards[6],
        shards[7],
        shards[8],
        shards[9],
        shards[10],
        shards[11],
    )


def solution(mesh):
    return jax.shard_map(
        local,
        mesh=mesh,
        in_specs=(
            P("fsdp", None),
            P("fsdp"),
            P("fsdp"),
            P("fsdp"),
            P("fsdp", None),
            P("fsdp"),
            P("fsdp", None),
            P("fsdp"),
            P("fsdp"),
            P("fsdp"),
            P("fsdp", None),
            P("fsdp"),
            P("fsdp", None),
            P("fsdp"),
            P("fsdp", None),
        ),
        out_specs=(
            P("fsdp", None),
            P("fsdp", None),
            P("fsdp"),
            P("fsdp"),
            P("fsdp", None),
            P("fsdp"),
            P("fsdp", None),
            P("fsdp"),
            P("fsdp"),
            P("fsdp"),
            P("fsdp", None),
            P("fsdp"),
            P("fsdp", None),
            P("fsdp"),
        ),
        check_vma=False,
    )
```

profile of v0, /device:TPU:0, one launch (start us, length us, event | category | flops | bytes accessed | tf_op | source)
XLA Modules:
  0.0 830.0 jit_solution(1642223400788358338)
XLA Ops:
  18.0 42.8 %all-reduce.19 = (bf16[1536]{0:T(1024)(128)(2,1)S(1)}, bf16[768]{0:T(1024)(128)(2,1)S(1)}, bf16[768]{0:T(1024)(128)(2,1)S(1)}, bf16[768]{0:T(1024)(128)(2,1)S(1)...) all-reduce(bf16[1536]{0:T(1024)(128)(2,1)S(1)} %dynamic-update-slic, ...), channel_id=1, replica_groups=mesh['fsdp'=32] {'fsdp'}, use_global_device_ids=true, to_apply=%add.4 | all-reduce | flops 9216 | bytes 36864
  68.6 5.2 all-gather.5.cloned.1.call-done
  73.8 6.4 add_convert_fusion
  103.7 6.0 fusion.47
  109.7 10.9 %fusion.1 = (f32[12,512]{1,0:T(8,128)S(1)}, f32[12,512,1024]{2,1,0:T(8,128)}) fusion(pred[512,1024]{1,0:T(8,128)(4,1)S(1)} %copy-done.17, bf16[512,12,64]{0,2,1:T(8,128)(2,1)S(1)} %bitcast.76, bf16[1024,12,64]{0,2,1:T(8,128)(2,1)S(1)} %bitcast.72), kind=kOutput, calls=%fused_computation.9 | convolution fusion | flops 824174592 | bytes 28073984 | tf_op jit(solution)/shard_map/qhd,khd->hqk/dot_general | solution.py:45
  123.2 13.5 %fusion = f32[12,512]{1,0:T(8,128)S(1)} fusion(f32[12,512,1024]{2,1,0:T(8,128)} %get-tuple-element.161, f32[12,512]{1,0:T(8,128)S(1)} %get-tuple-element.160, pred[512,1024]{1,0:T(8,128)(4,1)} %fusion.32), kind=kLoop, calls=%fused_computation.6 | loop fusion | flops 25159680 | bytes 25739264 | tf_op jit(solution)/shard_map/reduce_sum | solution.py:123
  139.2 9.7 %fusion.46 = bf16[512,12,64]{0,2,1:T(8,128)(2,1)} fusion(bf16[1024,12,64]{0,2,1:T(8,128)(2,1)} %bitcast.81, f32[12,512,1024]{2,1,0:T(8,128)S(1)} %copy-done, f32[12,512]{1,0:T(8,128)S(1)} %fusion, f32[12,512]{1,0:T(8,128)S(1)} %get-tuple-element.160, pred[512,1024]{1,0:T(8,128)(4,1)S(1)} %copy-done.18), kind=kOutput, calls=%fused_computation.83 | convolution fusion | flops 837156864 | bytes 28098560 | tf_op jit(solution)/shard_map/hqk,khd->qhd/dot_general | solution.py:126
  157.6 37.6 %all-gather.9.cloned.1.call-done = bf16[768,3072]{1,0:T(8,128)(2,1)} async-done(((bf16[24,3072]{1,0:T(8,128)(2,1)}), bf16[768,3072]{1,0:T(8,128)(2,1)}) %all-gather.9.cloned.1.call-update) | async-done | bytes 4718608 | tf_op jit(solution)/shard_map/all_gather | solution.py:88
  195.2 11.2 %fusion.68 = f32[1024,3072]{1,0:T(8,128)} fusion(bf16[768,3072]{1,0:T(8,128)(2,1)} %all-gather.9.cloned.1.call-done, f32[1024,768]{0,1:T(8,128)} %copy-done.5, f32[768]{0:T(1024)S(1)} %convert_element_type.150, f32[768]{0:T(1024)S(1)} %convert_element_type.149, f32[1024]{0:T(1024)S(1)} %fusion.52, f32[1024]{0:T(1024)S(1)} %broadcast_multiply_fusion), kind=kOutput, calls=%fused_computation.118 | convolution fusion | flops 4835770368 | bytes 20461568 | tf_op jit(solution)/shard_map/dot_general | solution.py:144
  206.3 54.1 %all-gather.11.cloned.1.call-done = bf16[3072,768]{1,0:T(8,128)(2,1)} async-done(((bf16[96,768]{1,0:T(8,128)(2,1)}), bf16[3072,768]{1,0:T(8,128)(2,1)}) %all-gather.11.cloned.1.call-update) | async-done | bytes 4718608 | tf_op jit(solution)/shard_map/all_gather | solution.py:90
  260.4 16.3 %convert_reduce_fusion = (f32[3072]{0:T(1024)}, bf16[1024,3072]{1,0:T(8,128)(2,1)S(1)}) fusion(f32[1024,3072]{1,0:T(8,128)} %fusion.68, f32[3072]{0:T(1024)S(1)} %copy-done.51, bf16[3072,768]{1,0:T(8,128)(2,1)} %all-gather.11.cloned.1.call-done, bf16[1024,768]{0,1:T(8,128)(2,1)S(1)} %copy.82, f32[1024]{0:T(1024)S(1)} %copy-done.45), kind=kOutput, calls=%fused_computation.17 | convolution fusion | flops 4906546176 | bytes 25194496 | tf_op jit(solution)/shard_map/dot_general | solution.py:31
  276.8 7.4 fusion.78
  284.2 3.7 copy.83
  299.3 8.2 fusion.38
  307.5 7.0 multiply_reduce_fusion.1
  314.7 10.0 %multiply_convert_fusion.1 = bf16[12,512,512]{1,2,0:T(8,128)(2,1)S(1)} fusion(f32[12,512,512]{1,2,0:T(8,128)} %get-tuple-element.167, f32[12,512]{1,0:T(8,128)S(1)} %get-tuple-element.166, f32[12,512]{1,0:T(8,128)S(1)} %copy-done.34, f32[12,512,512]{1,2,0:T(8,128)} %copy-done.1, pred[512,512]{0,1:T(8,128)(4,1)S(1)} %compare_and_fusion), kind=kLoop, calls=%fused_computation.20 | loop fusion | flops 22020096 | bytes 31768576 | tf_op jit(solution)/shard_map/convert_element_type | solution.py:206
  328.1 22.1 %multiply_reduce_fusion = (f32[12,512]{1,0:T(8,128)S(1)}, f32[12,512,1024]{2,1,0:T(8,128)}) fusion(f32[12,512]{1,0:T(8,128)S(1)} %log_add_fusion, f32[12,512,1024]{2,1,0:T(8,128)} %get-tuple-element.161, pred[512,1024]{1,0:T(8,128)(4,1)S(1)} %copy-done.19, bf16[512,12,64]{0,2,1:T(8,128)(2,1)S(1)} %bitcast.89, bf16[1024,12,64]{0,2,1:T(8,128)(2,1)S(1)} %bitcast.82), kind=kOutput, calls=%fused_computation.1 | convolution fusion | flops 843048960 | bytes 53264384 | tf_op jit(solution)/shard_map/qhd,khd->hqk/dot_general | solution.py:202
  350.2 18.2 %multiply_convert_fusion = bf16[12,512,1024]{2,1,0:T(8,128)(2,1)S(1)} fusion(f32[12,512,1024]{2,1,0:T(8,128)} %get-tuple-element.169, f32[12,512]{1,0:T(8,128)S(1)} %get-tuple-element.168, f32[12,512]{1,0:T(8,128)S(1)} %log_add_fusion, f32[12,512,1024]{2,1,0:T(8,128)} %get-tuple-element.161, pred[512,1024]{1,0:T(8,128)(4,1)} %fusion.32), kind=kLoop, calls=%fused_computation | loop fusion | flops 44040192 | bytes 63488000 | tf_op jit(solution)/shard_map/convert_element_type | solution.py:206
  368.4 6.2 multiply_bitcast_fusion.1
  374.7 5.2 fusion.29
  379.8 4.1 multiply_bitcast_fusion.2
  385.8 12.9 %convert_reduce_fusion.3 = (f32[12,64]{1,0:T(8,128)S(1)}, bf16[1024,12,64]{0,2,1:T(8,128)(2,1)S(1)}) fusion(bf16[512,12,64]{0,2,1:T(8,128)(2,1)S(1)} %bitcast.90, f32[12,512]{1,0:T(8,128)S(1)} %log_add_fusion, f32[12,512,1024]{2,1,0:T(8,128)} %get-tuple-element.161, pred[512,1024]{1,0:T(8,128)(4,1)S(1)} %copy-done.20, f32[512,12,64]{0,2,1:T(8,128)S(1)} %copy-done.61), kind=kOutput, calls=%fused_computation.58 | convolution fusion | flops 839908608 | bytes 29649920 | tf_op jit(solution)/shard_map/hqk,qhd->khd/dot_general | solution.py:223
  398.8 7.0 fusion.33
  407.3 14.1 %fusion.43 = f32[3072,768]{1,0:T(8,128)} fusion(bf16[1024,768]{0,1:T(8,128)(2,1)S(1)} %copy-done.13, f32[1024]{0:T(1024)S(1)} %copy-done.45, f32[1024,3072]{1,0:T(8,128)} %fusion.68, f32[3072]{0:T(1024)S(1)} %copy-done.51), kind=kOutput, calls=%fused_computation.82 | convolution fusion | flops 4865654784 | bytes 23609344 | tf_op jit(solution)/shard_map/dot_general | solution.py:25
  422.1 10.7 %fusion.67 = f32[768,3072]{1,0:T(8,128)} fusion(bf16[1024,3072]{1,0:T(8,128)(2,1)} %copy-done.60, f32[1024,768]{0,1:T(8,128)} %copy-done.5, f32[768]{0:T(1024)S(1)} %copy-done.33, f32[768]{0:T(1024)S(1)} %convert_element_type.149, f32[1024]{0:T(1024)S(1)} %fusion.52, f32[1024]{0:T(1024)S(1)} %broadcast_multiply_fusion), kind=kOutput, calls=%fused_computation.117 | convolution fusion | flops 4835770368 | bytes 18888704 | tf_op jit(solution)/shard_map/dot_general | solution.py:25
  433.5 12.7 %multiply_convert_fusion.3 = bf16[1024,768]{0,1:T(8,128)(2,1)} fusion(f32[1024,768]{0,1:T(8,128)} %copy-done.5, bf16[3072,768]{1,0:T(8,128)(2,1)} %all-gather.11.cloned.1.call-done, f32[768]{0:T(1024)S(1)} %convert_element_type.154, f32[1024]{0:T(1024)S(1)} %copy-done.45, f32[1024,3072]{1,0:T(8,128)} %fusion.68, f32[3072]{0:T(1024)S(1)} %copy-done.51), kind=kOutput, calls=%fused_computation.66 | convolution fusion | flops 4866441216 | bytes 22039552 | tf_op jit(solution)/shard_map/dot_general | solution.py:148
  448.9 9.3 %fusion.77 = (f32[768]{0:T(1024)S(1)}, f32[1024,768]{1,0:T(8,128)}) fusion(bf16[768,2304]{1,0:T(8,128)(2,1)} %all-gather.5.cloned.1.call-done, bf16[1024,768]{0,1:T(8,128)(2,1)} %bitcast.94, bf16[1024,768]{0,1:T(8,128)(2,1)} %bitcast.79, bf16[1024,768]{0,1:T(8,128)(2,1)} %bitcast.84), kind=kOutput, calls=%fused_computation.126 | convolution fusion | flops 3638820096 | bytes 11406336 | tf_op jit(solution)/shard_map/dot_general | solution.py:31
  458.1 3.8 copy.87
  470.0 42.2 %all-reduce.18 = (f32[768]{0:T(1024)S(1)}, f32[768]{0:T(1024)S(1)}, f32[1536]{0:T(1024)S(1)}, f32[768]{0:T(1024)S(1)}, f32[768]{0:T(1024)S(1)}, /*index=5*/f32[7...) all-reduce(f32[768]{0:T(1024)S(1)} %get-tuple-element.122, ...), channel_id=2, replica_groups=mesh['fsdp'=32] {'fsdp'}, use_global_device_ids=true, to_apply=%region_15.16.clone | all-reduce | flops 9216 | bytes 73728
  520.4 19.0 %reduce-scatter.5.cloned.1.call-done = f32[24,2304]{1,0:T(8,128)} async-done(((f32[768,2304]{1,0:T(8,128)}), f32[24,2304]{1,0:T(8,128)}) %reduce-scatter.5.cloned.1.call-update) | async-done | bytes 221200 | tf_op jit(solution)/shard_map/reduce_scatter | solution.py:254
  539.5 141.3 %reduce-scatter.11.cloned.1.call-done = f32[96,768]{1,0:T(8,128)} async-done(((f32[3072,768]{1,0:T(8,128)}), f32[96,768]{1,0:T(8,128)}) %reduce-scatter.11.cloned.1.call-update) | async-done | bytes 294928 | tf_op jit(solution)/shard_map/reduce_scatter | solution.py:262
  680.8 142.1 %reduce-scatter.9.cloned.1.call-done = f32[24,3072]{1,0:T(8,128)} async-done(((f32[768,3072]{1,0:T(8,128)}), f32[24,3072]{1,0:T(8,128)}) %reduce-scatter.9.cloned.1.call-update) | async-done | bytes 294928 | tf_op jit(solution)/shard_map/reduce_scatter | solution.py:260
  (236 shorter events, 93.2 us)
Async XLA Ops:
  7.2 66.6 %all-gather.5.cloned.1.call-start = ((), (), s32[]{:S(2)}) async-start(), calls=%async_computation.4 | async-start | bytes 3649536 | tf_op jit(solution)/shard_map/all_gather | solution.py:80
  7.9 143.5 %all-gather.7.cloned.1.call-start = ((), (), s32[]{:S(2)}) async-start(), calls=%async_computation.5 | async-start | bytes 1216512 | tf_op jit(solution)/shard_map/all_gather | solution.py:82
  8.7 186.5 %all-gather.9.cloned.1.call-start = ((), (), s32[]{:S(2)}) async-start(), calls=%async_computation.6 | async-start | bytes 4866048 | tf_op jit(solution)/shard_map/all_gather | solution.py:88
  9.4 251.0 %all-gather.11.cloned.1.call-start = ((), (), s32[]{:S(2)}) async-start(), calls=%async_computation.7 | async-start | bytes 4866048 | tf_op jit(solution)/shard_map/all_gather | solution.py:90
  10.0 510.5 %reduce-scatter.7.cloned.1.call-start = ((), (), s32[]{:S(2)}) async-start(), calls=%async_computation.9 | async-start | bytes 2433024 | tf_op jit(solution)/shard_map/reduce_scatter | solution.py:256
  11.3 53.3 %copy-start.48 = (s32[1024]{0:T(1024)}, s32[1024]{0:T(1024)S(1)}, u32[]{:S(2)}) copy-start(s32[1024]{0:T(1024)S(1)} %iota.22) | copy-start | bytes 12292
  60.8 13.0 %copy-start.37 = (f32[768]{0:T(1024)}, f32[768]{0:T(1024)S(1)}, u32[]{:S(2)}) copy-start(f32[768]{0:T(1024)S(1)} %convert_element_type.139) | copy-start | bytes 9220
  60.9 13.0 %copy-start.53 = (f32[768]{0:T(1024)}, f32[768]{0:T(1024)S(1)}, u32[]{:S(2)}) copy-start(f32[768]{0:T(1024)S(1)} %convert_element_type.140) | copy-start | bytes 9220
  60.9 134.3 %copy-start.32 = (f32[768]{0:T(1024)}, f32[768]{0:T(1024)S(1)}, u32[]{:S(2)}) copy-start(f32[768]{0:T(1024)S(1)} %convert_element_type.150) | copy-start | bytes 9220
  63.8 87.6 %copy-start.3 = (bf16[1024,768]{0,1:T(8,128)(2,1)}, bf16[1024,768]{0,1:T(8,128)(2,1)S(1)}, u32[]{:S(2)}) copy-start(bf16[1024,768]{0,1:T(8,128)(2,1)S(1)} %copy.73) | copy-start | bytes 4718596
  64.1 16.1 %copy-start.35 = (f32[1024]{0:T(1024)}, f32[1024]{0:T(1024)S(1)}, u32[]{:S(2)}) copy-start(f32[1024]{0:T(1024)S(1)} %broadcast_multiply_fusion.1) | copy-start | bytes 12292
  65.2 15.1 %copy-start.39 = (f32[1024]{0:T(1024)}, f32[1024]{0:T(1024)S(1)}, u32[]{:S(2)}) copy-start(f32[1024]{0:T(1024)S(1)} %fusion.51) | copy-start | bytes 12292
  66.9 193.5 %copy-start.11 = (bf16[1024,768]{0,1:T(8,128)(2,1)}, bf16[1024,768]{0,1:T(8,128)(2,1)S(1)}, u32[]{:S(2)}) copy-start(bf16[1024,768]{0,1:T(8,128)(2,1)S(1)} %copy.82) | copy-start | bytes 4718596
  123.2 16.0 %copy-start = (f32[12,512,1024]{2,1,0:T(8,128)S(1)}, f32[12,512,1024]{2,1,0:T(8,128)}, u32[]{:S(2)}) copy-start(f32[12,512,1024]{2,1,0:T(8,128)} %get-tuple-element.161) | copy-start | bytes 75497472
  123.2 16.0 %copy-start.18 = (pred[512,1024]{1,0:T(8,128)(4,1)S(1)}, pred[512,1024]{1,0:T(8,128)(4,1)}, u32[]{:S(2)}) copy-start(pred[512,1024]{1,0:T(8,128)(4,1)} %fusion.32) | copy-start | bytes 1572868
  139.2 9.7 %copy-start.31 = (bf16[512,12,64]{0,2,1:T(8,128)(2,1)S(1)}, bf16[512,12,64]{0,2,1:T(8,128)(2,1)}, u32[]{:S(2)}) copy-start(bf16[512,12,64]{0,2,1:T(8,128)(2,1)} %fusion.47) | copy-start | bytes 2359300
  157.6 102.9 %copy-start.45 = (f32[1024]{0:T(1024)S(1)}, f32[1024]{0:T(1024)}, u32[]{:S(2)}) copy-start(f32[1024]{0:T(1024)} %fusion.49) | copy-start | bytes 12292
  157.6 102.8 %copy-start.51 = (f32[3072]{0:T(1024)S(1)}, f32[3072]{0:T(1024)}, u32[]{:S(2)}) copy-start(f32[3072]{0:T(1024)} %convert_element_type.152) | copy-start | bytes 36868
  260.4 16.4 %copy-start.22 = (bf16[768,3072]{1,0:T(8,128)(2,1)S(1)}, bf16[768,3072]{1,0:T(8,128)(2,1)}, u32[]{:S(2)}) copy-start(bf16[768,3072]{1,0:T(8,128)(2,1)} %all-gather.9.cloned.1.call-done) | copy-start | bytes 14155780
  297.8 9.7 %slice-start = ((s8[12582912]{0:T(1024)(128)(4,1)}), s8[4194304]{0:T(1024)(128)(4,1)S(1)}, s32[]{:S(2)}) async-start(s8[12582912]{0:T(1024)(128)(4,1)} %bitcast.69), calls=%async_computation.12 | async-start | bytes 8388608
  299.3 28.8 %copy-start.29 = (bf16[512,768]{0,1:T(8,128)(2,1)}, bf16[512,768]{0,1:T(8,128)(2,1)S(1)}, u32[]{:S(2)}) copy-start(bf16[512,768]{0,1:T(8,128)(2,1)S(1)} %get-tuple-element.154) | copy-start | bytes 2359300
  314.6 224.9 %reduce-scatter.5.cloned.1.call-start = ((), (), s32[]{:S(2)}) async-start(), calls=%async_computation.8 | async-start | bytes 7299072 | tf_op jit(solution)/shard_map/reduce_scatter | solution.py:254
  314.6 10.1 %copy-start.21 = (bf16[512,768]{0,1:T(8,128)(2,1)S(1)}, bf16[512,768]{0,1:T(8,128)(2,1)}, u32[]{:S(2)}) copy-start(bf16[512,768]{0,1:T(8,128)(2,1)} %copy.75) | copy-start | bytes 2359300
  385.8 12.9 %copy-start.26 = (bf16[1024,12,64]{0,2,1:T(8,128)(2,1)}, bf16[1024,12,64]{0,2,1:T(8,128)(2,1)S(1)}, u32[]{:S(2)}) copy-start(bf16[1024,12,64]{0,2,1:T(8,128)(2,1)S(1)} %get-tuple-element.143) | copy-start | bytes 4718596
  385.8 12.9 %copy-start.4 = (bf16[1024,768]{0,1:T(8,128)(2,1)S(1)}, bf16[1024,768]{0,1:T(8,128)(2,1)}, u32[]{:S(2)}) copy-start(bf16[1024,768]{0,1:T(8,128)(2,1)} %copy-done.3) | copy-start | bytes 4718596
  385.8 12.9 %copy-start.24 = (bf16[1024,12,64]{0,2,1:T(8,128)(2,1)S(1)}, bf16[1024,12,64]{0,2,1:T(8,128)(2,1)}, u32[]{:S(2)}) copy-start(bf16[1024,12,64]{0,2,1:T(8,128)(2,1)} %fusion.29) | copy-start | bytes 4718596
  385.8 13.0 %copy-start.36 = (f32[1024]{0:T(1024)S(1)}, f32[1024]{0:T(1024)}, u32[]{:S(2)}) copy-start(f32[1024]{0:T(1024)} %copy-done.35) | copy-start | bytes 12292
  385.8 13.0 %copy-start.38 = (f32[768]{0:T(1024)S(1)}, f32[768]{0:T(1024)}, u32[]{:S(2)}) copy-start(f32[768]{0:T(1024)} %copy-done.37) | copy-start | bytes 9220
  385.8 13.0 %copy-start.40 = (f32[1024]{0:T(1024)S(1)}, f32[1024]{0:T(1024)}, u32[]{:S(2)}) copy-start(f32[1024]{0:T(1024)} %copy-done.39) | copy-start | bytes 12292
  385.8 13.0 %copy-start.54 = (f32[768]{0:T(1024)S(1)}, f32[768]{0:T(1024)}, u32[]{:S(2)}) copy-start(f32[768]{0:T(1024)} %copy-done.53) | copy-start | bytes 9220
  405.9 274.9 %reduce-scatter.11.cloned.1.call-start = ((), (), s32[]{:S(2)}) async-start(), calls=%async_computation.11 | async-start | bytes 9732096 | tf_op jit(solution)/shard_map/reduce_scatter | solution.py:262
  421.4 401.5 %reduce-scatter.9.cloned.1.call-start = ((), (), s32[]{:S(2)}) async-start(), calls=%async_computation.10 | async-start | bytes 9732096 | tf_op jit(solution)/shard_map/reduce_scatter | solution.py:260
  (42 other events, 140.6 us)
Sparse Core Ops, SparseCore 0:
  10.9 62.8 all-gather.4
  76.7 52.8 all-gather.6
  132.6 62.5 all-gather.8
  197.9 62.4 all-gather.10
  314.7 97.8 reduce-scatter.6
  419.7 119.7 reduce-scatter.4
  545.9 134.8 reduce-scatter.10
  688.3 134.6 reduce-scatter.8
where the time goes:
time: 841 us; the launch traced here: 830 us
  waiting for transfers between devices  402 us (48%)
  matrix products  202 us (24%)
  blocking collectives  85 us (10%)
  other arithmetic  65.3 us (8%)
  local copies, waits for them, and re-layouts  59.9 us (7%)
  between operations  15.8 us (2%)
    reduce_scatter x1, waiting for transfers between devices, local(): lax.psum_scatter(grad_w_up, 'fsdp', scatter_dimension=0, tiled=True)  142 us
    reduce_scatter x1, waiting for transfers between devices, local(): lax.psum_scatter(grad_w_down, 'fsdp', scatter_dimension=0, tiled=True)  141 us
    unnamed x2, blocking collectives  85 us
    all_gather x1, waiting for transfers between devices, local(): lax.all_gather(w_down, 'fsdp', axis=0, tiled=True)  54.1 us
    all_gather x1, waiting for transfers between devices, local(): lax.all_gather(w_up, 'fsdp', axis=0, tiled=True)  37.6 us
    dot_general x4, matrix products, weight_grad(): lax.dot_general(left, right, (((0,), (0,)), ((), ())), preferred_element_...  34.8 us
    dot_general x4, matrix products, back_product(): lax.dot_general(grad_low, weight, (((1,), (1,)), ((), ())), preferred_ele...  34.4 us
    unnamed x159, local copies, waits for them, and re-layouts  34 us
  transfers between devices with their start and end apart: 8, of which 6 were waited for; matrix products, arithmetic and copies ran while one was open for 31% of the time, Pallas kernels for 0%

commit v1 on v0

v1 whole, which is shorter than its diff:
```python
import functools

import jax
import jax.numpy as jnp
from jax import lax
from jax.experimental import pallas as pl
from jax.experimental.pallas import tpu as pltpu
from jax.sharding import PartitionSpec as P

HEAD_DIM = 64


EPSILON = 1e-05
NEG_FILL = -1e30


def normalize(values, gain_vec, shift_vec):
    row_mean = jnp.mean(values, axis=-1, keepdims=True)
    centred = values - row_mean
    variance = jnp.mean(centred * centred, axis=-1, keepdims=True)
    return centred * lax.rsqrt(variance + EPSILON) * gain_vec + shift_vec


def gelu_tanh(values):
    return jax.nn.gelu(values, approximate=True)


def weight_grad(left, right):
    return lax.dot_general(
        left, right, (((0,), (0,)), ((), ())), preferred_element_type=jnp.float32
    )


def back_product(grad_low, weight):
    return lax.dot_general(
        grad_low, weight, (((1,), (1,)), ((), ())), preferred_element_type=jnp.float32
    )


LANES = 128
NT = (((1,), (1,)), ((), ()))
TN = (((0,), (0,)), ((), ()))


def dot32(left, right, dims=(((1,), (0,)), ((), ()))):
    return lax.dot_general(left, right, dims, preferred_element_type=jnp.float32)


def head_masks(rows):
    lane = lax.broadcasted_iota(jnp.int32, (rows, LANES), 1)
    return lane < HEAD_DIM


def pick(mask, array, head):
    zero = jnp.zeros_like(array)
    return jnp.where(mask, array, zero) if head == 0 else jnp.where(mask, zero, array)


def attend_kernel(block, q_ref, k_ref, v_ref, out_ref, lse_ref):
    rows = q_ref.shape[0]
    scale_value = HEAD_DIM ** (-0.5)
    mask = head_masks(rows)
    keys = k_ref[...]
    values = v_ref[...]
    keys_of = [pick(mask, keys, head) for head in range(2)]
    values_of = [pick(mask, values, head) for head in range(2)]
    for start in range(0, rows, block):
        stop = start + block
        queries = q_ref[start:stop, :] * jnp.bfloat16(scale_value)
        total = None
        for head in range(2):
            scores = dot32(queries, keys_of[head][:stop], NT)
            row = lax.broadcasted_iota(jnp.int32, scores.shape, 0) + start
            column = lax.broadcasted_iota(jnp.int32, scores.shape, 1)
            scores = jnp.where(column <= row, scores, NEG_FILL)
            row_top = jnp.max(scores, axis=-1, keepdims=True)
            exp_scores = jnp.exp(scores - row_top)
            row_total = jnp.sum(exp_scores, axis=-1, keepdims=True)
            probs_low = (exp_scores * (1.0 / row_total)).astype(jnp.bfloat16)
            part = dot32(probs_low, values_of[head][:stop])
            total = part if total is None else total + part
            lse = jnp.broadcast_to(row_top + jnp.log(row_total), (block, LANES))
            lse_ref[0, head : head + 1, start:stop] = lse.T[:1]
        out_ref[start:stop, :] = total.astype(jnp.bfloat16)


def attend_back_kernel(
    block, q_ref, k_ref, v_ref, out_ref, lse_ref, grad_ref, dq_ref, dk_ref, dv_ref, dk_sum, dv_sum
):
    rows = q_ref.shape[0]
    scale_value = HEAD_DIM ** (-0.5)
    mask = head_masks(rows)
    keys = k_ref[...]
    values = v_ref[...]
    keys_of = [pick(mask, keys, head) for head in range(2)]
    values_of = [pick(mask, values, head) for head in range(2)]
    dk_sum[...] = jnp.zeros_like(dk_sum)
    dv_sum[...] = jnp.zeros_like(dv_sum)
    for start in range(0, rows, block):
        stop = start + block
        queries = q_ref[start:stop, :] * jnp.bfloat16(scale_value)
        grad = grad_ref[start:stop, :]
        turned = (grad.astype(jnp.float32) * out_ref[start:stop, :].astype(jnp.float32)).T
        grad_q = None
        for head in range(2):
            row_delta = jnp.sum(
                turned[head * HEAD_DIM : (head + 1) * HEAD_DIM], axis=0, keepdims=True
            )
            lse = lse_ref[0, head : head + 1, start:stop]
            scores = dot32(keys_of[head][:stop], queries, NT)
            key_pos = lax.broadcasted_iota(jnp.int32, scores.shape, 0)
            query_pos = lax.broadcasted_iota(jnp.int32, scores.shape, 1) + start
            probs = jnp.where(key_pos <= query_pos, jnp.exp(scores - lse), 0.0)
            grad_probs = dot32(values_of[head][:stop], grad, NT)
            grad_scores = (probs * (grad_probs - row_delta)).astype(jnp.bfloat16)
            dv_sum[:stop, :] += dot32(probs.astype(jnp.bfloat16), pick(mask[:block], grad, head))
            dk_sum[:stop, :] += dot32(grad_scores, pick(mask[:block], queries, head))
            part = dot32(grad_scores, keys_of[head][:stop], TN)
            grad_q = part if grad_q is None else grad_q + part
        dq_ref[start:stop, :] = (grad_q * scale_value).astype(jnp.bfloat16)
    dk_ref[...] = dk_sum[...].astype(jnp.bfloat16)
    dv_ref[...] = dv_sum[...].astype(jnp.bfloat16)


def column_spec(rows, offset):
    return pl.BlockSpec((rows, LANES), lambda pair: (0, offset + pair))


def lse_spec(rows):
    return pl.BlockSpec((1, 8, rows), lambda pair: (pair, 0, 0))


def attend(qkv_low):
    rows, width = qkv_low.shape[0], qkv_low.shape[1] // 3
    pairs = width // LANES
    block = min(256, rows)
    return pl.pallas_call(
        functools.partial(attend_kernel, block),
        grid=(pairs,),
        in_specs=[column_spec(rows, pairs * part) for part in range(3)],
        out_specs=[column_spec(rows, 0), lse_spec(rows)],
        out_shape=[
            jax.ShapeDtypeStruct((rows, width), jnp.bfloat16),
            jax.ShapeDtypeStruct((pairs, 8, rows), jnp.float32),
        ],
        compiler_params=pltpu.CompilerParams(vmem_limit_bytes=40 * 1024 * 1024),
        cost_estimate=pl.CostEstimate(
            flops=4 * rows * rows * width, bytes_accessed=8 * rows * width, transcendentals=0
        ),
    )(qkv_low, qkv_low, qkv_low)


def attend_back(qkv_low, attended, lse, grad_attended):
    rows, width = attended.shape
    pairs = width // LANES
    block = min(256, rows)
    return pl.pallas_call(
        functools.partial(attend_back_kernel, block),
        grid=(pairs,),
        in_specs=[column_spec(rows, pairs * part) for part in range(3)]
        + [column_spec(rows, 0), lse_spec(rows), column_spec(rows, 0)],
        out_specs=[column_spec(rows, 0)] * 3,
        out_shape=[jax.ShapeDtypeStruct((rows, width), jnp.bfloat16)] * 3,
        scratch_shapes=[pltpu.VMEM((rows, LANES), jnp.float32)] * 2,
        compiler_params=pltpu.CompilerParams(vmem_limit_bytes=40 * 1024 * 1024),
        cost_estimate=pl.CostEstimate(
            flops=10 * rows * rows * width, bytes_accessed=16 * rows * width, transcendentals=0
        ),
    )(qkv_low, qkv_low, qkv_low, attended, lse, grad_attended)


def fold(shard, width):
    rows, columns = shard.shape
    return shard.reshape(rows, columns // width, width).transpose(1, 0, 2).reshape(-1, width)


def unfold(stacked, count):
    parts, rows, width = stacked.shape
    each = rows // count
    return (
        stacked.reshape(parts, count, each, width)
        .transpose(0, 2, 1, 3)
        .reshape(parts * each, count * width)
    )


def fold_all(full, parts, width):
    rows = full.shape[0] // parts
    count = full.shape[1] // width
    return (
        full.reshape(parts, rows, count, width)
        .transpose(0, 2, 1, 3)
        .reshape(parts, count * rows, width)
    )


def unfold_one(stacked, count):
    return unfold(stacked[None], count)


def local(
    hidden_in,
    lengths,
    ln1_gain,
    ln1_bias,
    w_qkv,
    b_qv,
    w_out,
    b_out,
    ln2_gain,
    ln2_bias,
    w_up,
    b_up,
    w_down,
    b_down,
    cotangent,
):
    token_count = hidden_in.shape[0]
    model_width = hidden_in.shape[1]
    parts = lax.axis_size("fsdp")
    vectors = (ln1_gain, ln1_bias, b_qv, b_out, ln2_gain, ln2_bias, b_up, b_down)
    joined = jnp.concatenate(vectors)
    vector_rows = 16
    vector_pad = jnp.zeros((vector_rows, model_width), jnp.bfloat16)
    vector_block = lax.dynamic_update_slice(vector_pad, joined[None], (0, 0))
    own_rows = w_qkv.shape[0]

    def gathered(pieces):
        stacked = jnp.concatenate(pieces, axis=0)
        whole = lax.all_gather(stacked, "fsdp", axis=0, tiled=True)
        return whole.reshape(parts, stacked.shape[0], model_width)

    first = gathered([fold(w_qkv, model_width), vector_block])
    qkv_rows = 3 * own_rows
    qkv_weight = unfold(first[:, :qkv_rows], 3)
    full_vectors = []
    offset = 0
    for vector in vectors:
        size = vector.shape[0]
        full_vectors.append(
            first[:, qkv_rows, offset : offset + size].reshape(-1).astype(jnp.float32)
        )
        offset += size
    gain_one, shift_one, qv_bias, out_bias, gain_two, shift_two, up_bias, down_bias = full_vectors
    up_count = w_up.shape[1] // model_width
    second = gathered([w_out, fold(w_up, model_width), w_down])
    out_weight = second[:, :own_rows].reshape(-1, model_width)
    up_rows = own_rows * up_count
    up_weight = unfold(second[:, own_rows : own_rows + up_rows], up_count)
    down_weight = second[:, own_rows + up_rows :].reshape(-1, model_width)

    positions = jnp.arange(token_count, dtype=jnp.int32)
    live_mask = (positions < lengths[0]).astype(jnp.float32)[:, None]
    inputs = hidden_in.astype(jnp.float32)
    normed_one, norm_one_back = jax.vjp(normalize, inputs, gain_one, shift_one)
    normed_one = normed_one.astype(jnp.bfloat16)
    bias_full = jnp.concatenate(
        [qv_bias[:model_width], jnp.zeros((model_width,), jnp.float32), qv_bias[model_width:]]
    )
    qkv_low = (
        jnp.dot(normed_one, qkv_weight, preferred_element_type=jnp.float32) + bias_full
    ).astype(jnp.bfloat16)
    attended, lse = attend(qkv_low)
    middle = inputs + (
        jnp.dot(attended, out_weight, preferred_element_type=jnp.float32) + out_bias
    )
    normed_two, norm_two_back = jax.vjp(normalize, middle, gain_two, shift_two)
    normed_two = normed_two.astype(jnp.bfloat16)
    hidden_pre = jnp.dot(normed_two, up_weight, preferred_element_type=jnp.float32) + up_bias
    activated = gelu_tanh(hidden_pre).astype(jnp.bfloat16)
    mlp_out = jnp.dot(activated, down_weight, preferred_element_type=jnp.float32) + down_bias
    output = (live_mask * (middle + mlp_out)).astype(jnp.bfloat16)

    grad_out = cotangent.astype(jnp.float32) * live_mask
    grad_out_low = grad_out.astype(jnp.bfloat16)
    grad_w_down = weight_grad(activated, grad_out_low).astype(jnp.bfloat16)
    grad_b_down = jnp.sum(grad_out, axis=0)
    grad_act = back_product(grad_out_low, down_weight)
    gelu_back = jax.vjp(gelu_tanh, hidden_pre)[1]
    grad_hidden = gelu_back(grad_act)[0].astype(jnp.bfloat16)
    grad_w_up = weight_grad(normed_two, grad_hidden).astype(jnp.bfloat16)
    grad_b_up = jnp.sum(grad_hidden.astype(jnp.float32), axis=0)

    def scattered(pieces):
        stacked = jnp.concatenate(pieces, axis=1)
        flat = stacked.reshape(-1, model_width)
        return lax.psum_scatter(flat, "fsdp", scatter_dimension=0, tiled=True)

    mlp_shard = scattered(
        [
            fold_all(grad_w_up, parts, model_width),
            grad_w_down.reshape(parts, -1, model_width),
        ]
    ).astype(jnp.float32)

    grad_middle_norm, grad_ln2_gain, grad_ln2_bias = norm_two_back(
        back_product(grad_hidden, up_weight)
    )
    grad_middle = grad_out + grad_middle_norm
    grad_attn_low = grad_middle.astype(jnp.bfloat16)
    grad_w_out = weight_grad(attended, grad_attn_low).astype(jnp.bfloat16)
    grad_b_out = jnp.sum(grad_attn_low.astype(jnp.float32), axis=0)
    grad_attended = back_product(grad_attn_low, out_weight).astype(jnp.bfloat16)
    grad_parts = attend_back(qkv_low, attended, lse, grad_attended)
    grad_qkv = jnp.concatenate(grad_parts, axis=1)
    grad_w_qkv = [weight_grad(normed_one, part).astype(jnp.bfloat16) for part in grad_parts]
    grad_b_qv = jnp.concatenate(
        [
            jnp.sum(grad_parts[0].astype(jnp.float32), axis=0),
            jnp.sum(grad_parts[2].astype(jnp.float32), axis=0),
        ]
    )
    grad_in_norm, grad_ln1_gain, grad_ln1_bias = norm_one_back(
        back_product(grad_qkv, qkv_weight)
    )
    grad_inputs = grad_middle + grad_in_norm
    vector_grads = (
        grad_ln1_gain,
        grad_ln1_bias,
        grad_b_qv,
        grad_b_out,
        grad_ln2_gain,
        grad_ln2_bias,
        grad_b_up,
        grad_b_down,
    )
    vector_rows_grad = jnp.concatenate([g.reshape(parts, -1) for g in vector_grads], axis=1)
    vector_rows_grad = vector_rows_grad.astype(jnp.bfloat16)[:, None, :]
    padded = jnp.pad(
        vector_rows_grad,
        ((0, 0), (0, vector_rows - 1), (0, model_width - vector_rows_grad.shape[2])),
    )
    attn_shard = scattered(
        [part.reshape(parts, -1, model_width) for part in grad_w_qkv]
        + [grad_w_out.reshape(parts, -1, model_width), padded]
    ).astype(jnp.float32)
    grad_vector_shards = []
    offset = 0
    for vector in vectors:
        size = vector.shape[0]
        grad_vector_shards.append(attn_shard[4 * own_rows, offset : offset + size])
        offset += size
    g_ln1g, g_ln1b, g_bqv, g_bout, g_ln2g, g_ln2b, g_bup, g_bdown = grad_vector_shards
    return (
        output,
        grad_inputs,
        g_ln1g,
        g_ln1b,
        unfold_one(attn_shard[:qkv_rows], 3),
        g_bqv,
        attn_shard[qkv_rows : qkv_rows + own_rows],
        g_bout,
        g_ln2g,
        g_ln2b,
        unfold_one(mlp_shard[:up_rows], up_count),
        g_bup,
        mlp_shard[up_rows:],
        g_bdown,
    )


def solution(mesh):
    return jax.shard_map(
        local,
        mesh=mesh,
        in_specs=(
            P("fsdp", None),
            P("fsdp"),
            P("fsdp"),
            P("fsdp"),
            P("fsdp", None),
            P("fsdp"),
            P("fsdp", None),
            P("fsdp"),
            P("fsdp"),
            P("fsdp"),
            P("fsdp", None),
            P("fsdp"),
            P("fsdp", None),
            P("fsdp"),
            P("fsdp", None),
        ),
        out_specs=(
            P("fsdp", None),
            P("fsdp", None),
            P("fsdp"),
            P("fsdp"),
            P("fsdp", None),
            P("fsdp"),
            P("fsdp", None),
            P("fsdp"),
            P("fsdp"),
            P("fsdp"),
            P("fsdp", None),
            P("fsdp"),
            P("fsdp", None),
            P("fsdp"),
        ),
        check_vma=False,
    )
```

time: 841 us -> 559 us (0.66)
  matrix products: 202 us -> 89.1 us
  waiting for transfers between devices: 402 us -> 291 us
  blocking collectives: 85 us -> 0 us
  Pallas kernels: 0 us -> 44.8 us
  other arithmetic: 65.3 us -> 25.7 us
  local copies, waits for them, and re-layouts: 59.9 us -> 84.6 us
    reduce_scatter x4 -> x2, waiting for transfers between devices: 303 us -> 186 us  [scattered(): return lax.psum_scatter(flat, 'fsdp', scatter_dimension=0, tiled=True)]
    dot_general x14 -> x2, matrix products: 114 us -> 10.2 us  [the longest x1 8.51 us: local(): jnp.dot(normed_two, up_weight, preferred_element_type=jnp.float32) + up_bias]
    unnamed x2 -> x0, blocking collectives: 85 us -> none
    pallas_call x0 -> x2, Pallas kernels: none -> 44.8 us  [the longest x1 25.4 us: attend_back(): pl.pallas_call(functools.partial(attend_back_kernel, block), grid=(pairs,...]
    convert_element_type x12 -> x5, other arithmetic: 30.1 us -> 5 us  [the longest x3 4.06 us: local(): first[:, qkv_rows, offset:offset + size].reshape(-1).astype(jnp.float32)]
    reduce_sum x3 -> x2, other arithmetic: 16.3 us -> 0.58 us  [the longest x1 0.29 us: local(): jnp.sum(grad_parts[0].astype(jnp.float32), axis=0)]
    reshape x0 -> x4, local copies, waits for them, and re-layouts: none -> 15.2 us  [the longest x2 13.4 us: fold_all(): full.reshape(parts, rows, count, width).transpose(0, 2, 1, 3)]
    all_gather x4 -> x2, waiting for transfers between devices: 96.9 us -> 104 us  [gathered(): whole = lax.all_gather(stacked, 'fsdp', axis=0, tiled=True)]
  transfers between devices with their start and end apart: 8 -> 4, of which waited for: 6 -> 4; matrix products, arithmetic and copies ran while one was open for 31% -> 16% of each run, Pallas kernels for 0% -> 4%
where the time goes in v1:
time: 559 us; the launch traced here: 551 us
  waiting for transfers between devices  291 us (52%)
  matrix products  89.1 us (16%)
  local copies, waits for them, and re-layouts  84.6 us (15%)
  Pallas kernels  44.8 us (8%)
  other arithmetic  25.7 us (5%)
  between operations  15.3 us (3%)
    reduce_scatter x2, waiting for transfers between devices, scattered(): return lax.psum_scatter(flat, 'fsdp', scatter_dimension=0, tiled=True)  186 us
    all_gather x2, waiting for transfers between devices, gathered(): whole = lax.all_gather(stacked, 'fsdp', axis=0, tiled=True)  104 us
    dot_general x6, matrix products, weight_grad(): lax.dot_general(left, right, (((0,), (0,)), ((), ())), preferred_element_...  33.7 us
    dot_general x4, matrix products, back_product(): lax.dot_general(grad_low, weight, (((1,), (1,)), ((), ())), preferred_ele...  28.9 us
    unnamed x75, local copies, waits for them, and re-layouts  28.7 us
    pallas_call x1, Pallas kernels, attend_back(): pl.pallas_call(functools.partial(attend_back_kernel, block), grid=(pairs,...  25.4 us
    pallas_call x1, Pallas kernels, attend(): pl.pallas_call(functools.partial(attend_kernel, block), grid=(pairs,), in...  19.4 us
    reshape x2, local copies, waits for them, and re-layouts, fold_all(): full.reshape(parts, rows, count, width).transpose(0, 2, 1, 3)  13.4 us
  transfers between devices with their start and end apart: 4, of which 4 were waited for; matrix products, arithmetic and copies ran while one was open for 16% of the time, Pallas kernels for 4%

profile of v1, /device:TPU:0, one launch (start us, length us, event | category | flops | bytes accessed | tf_op | source)
XLA Modules:
  0.0 550.6 jit_solution(556780300691174863)
XLA Ops:
  7.2 5.5 %concatenate.57 = bf16[288]{0:T(512)(128)(2,1)S(1)} concatenate(bf16[24]{0:T(256)(128)(2,1)} %param.17, bf16[24]{0:T(256)(128)(2,1)} %param.18, bf16[48]{0:T(256)(128)(2,1)} %param.20, bf16[24]{0:T(256)(128)(2,1)} %param.22, bf16[24]{0:T(256)(128)(2,1)} %param.23, bf16[24]{0:T(256)(128)(2,1)} %param.24, bf16[96]{0:T(256)(128)(2,1)} %param.26, bf16[24]{0:T(256)(128)(2,1)} %param.28), dimensions={0} | concatenate | bytes 1152 | tf_op jit(solution)/shard_map/concatenate | solution.py:222
  18.6 3.2 copy.68
  22.5 57.4 %all-gather.3.cloned.1.call-done = bf16[2816,768]{1,0:T(8,128)(2,1)} async-done(((bf16[88,768]{1,0:T(8,128)(2,1)}), bf16[2816,768]{1,0:T(8,128)(2,1)}) %all-gather.3.cloned.1.call-update) | async-done | bytes 4325392 | tf_op jit(solution)/shard_map/all_gather | solution.py:230
  79.8 4.0 slice.114
  88.6 4.5 copy.64
  95.8 4.6 add_convert_fusion.q_ref.k_ref.v_ref
  100.3 19.4 %shard_map.254 = (bf16[1024,768]{1,0:T(8,128)(2,1)S(1)}, f32[6,8,1024]{2,1,0:T(8,128)S(1)}) custom-call(bf16[1024,2304]{1,0:T(8,128)(2,1)S(1)} %add_convert_fusion.q_ref.k_ref.v_ref, bf16[1024,2304]{1,0:T(8,128)(2,1)S(1)} %add_convert_fusion.q_ref.k_ref.v_ref, bf16[1024,2304]{1,0:T(8,128)(2,1)S(1)} %add_convert_fusion.q_ref.k_ref.v_ref), custom_call_target="tpu_custom_call" | custom-call | flops 3221225472 | bytes 6291456 | tf_op jit(solution)/shard_map/pallas_call | solution.py:137
  121.9 47.1 %all-gather.5.cloned.1.call-done = bf16[6912,768]{1,0:T(8,128)(2,1)} async-done(((bf16[216,768]{1,0:T(8,128)(2,1)}), bf16[6912,768]{1,0:T(8,128)(2,1)}) %all-gather.5.cloned.1.call-update) | async-done | bytes 10616848 | tf_op jit(solution)/shard_map/all_gather | solution.py:230
  170.4 6.9 %fusion.51 = (bf16[32,96,768]{2,1,0:T(8,128)(2,1)S(1)}, bf16[32,96,768]{2,1,0:T(8,128)(2,1)}) fusion(bf16[32,216,768]{2,1,0:T(8,128)(2,1)} %bitcast.94), kind=kLoop, calls=%fused_computation.106 | loop fusion | bytes 18874368 | tf_op jit(solution)/shard_map/slice | solution.py:249
  182.9 8.5 %fusion.43 = f32[1024,3072]{1,0:T(8,128)} fusion(bf16[768,3072]{1,0:T(8,128)(2,1)S(1)} %bitcast.86, f32[1024,768]{0,1:T(8,128)S(1)} %get-tuple-element.95, f32[768]{0:T(1024)S(1)} %reshape.380, f32[768]{0:T(1024)S(1)} %reshape.379, f32[1024]{0:T(1024)S(1)} %fusion.41, f32[1024]{0:T(1024)S(1)} %broadcast_multiply_fusion), kind=kOutput, calls=%fused_computation.103 | convolution fusion | flops 4835770368 | bytes 20461568 | tf_op jit(solution)/shard_map/dot_general | solution.py:269
  191.4 15.0 %fusion.56 = (bf16[3072]{0:T(1024)(128)(2,1)S(1)}, bf16[1024,3072]{1,0:T(8,128)(2,1)S(1)}) fusion(f32[1024,3072]{1,0:T(8,128)} %fusion.43, f32[3072]{0:T(1024)S(1)} %reshape.381, bf16[3072,768]{1,0:T(8,128)(2,1)S(1)} %bitcast.98, bf16[1024,768]{0,1:T(8,128)(2,1)S(1)} %copy-done.13, f32[1024]{0:T(1024)S(1)} %fusion.39), kind=kOutput, calls=%fused_computation.111 | convolution fusion | flops 4903400448 | bytes 25188352 | tf_op jit(solution)/shard_map/dot_general | solution.py:35
  206.4 6.8 %fusion.55 = (bf16[768]{0:T(1024)(128)(2,1)S(1)}, f32[1024,768]{1,0:T(8,128)}) fusion(bf16[1024,3072]{1,0:T(8,128)(2,1)S(1)} %get-tuple-element.101, bf16[768,3072]{1,0:T(8,128)(2,1)S(1)} %bitcast.87), kind=kOutput, calls=%fused_computation.110 | convolution fusion | flops 4832623616 | bytes 14157312 | tf_op jit(solution)/shard_map/dot_general | solution.py:35
  213.3 3.6 copy.69
  216.8 3.9 multiply_reduce_fusion
  226.0 2.5 convolution_convert_fusion.3
  229.9 25.4 %shard_map.255 = (bf16[1024,768]{1,0:T(8,128)(2,1)S(1)}, bf16[1024,768]{1,0:T(8,128)(2,1)S(1)}, bf16[1024,768]{1,0:T(8,128)(2,1)S(1)}) custom-call(bf16[1024,2304]{1,0:T(8,128)(2,1)S(1)} %bitcast.84, bf16[1024,2304]{1,0:T(8,128)(2,1)S(1)} %bitcast.84, bf16[1024,2304]{1,0:T(8,128)(2,1)S(1)} %bitcast.84, bf16[1024,768]{1,0:T(8,128)(2,1)S(1)} %copy-done.2, ...), custom_call_target="tpu_custom_call" | custom-call | flops 8053063680 | bytes 12582912 | tf_op jit(solution)/shard_map/pallas_call | solution.py:157
  255.3 2.6 convolution_convert_fusion.5
  257.9 2.6 convolution_convert_fusion.6
  260.5 5.6 %fusion.54 = (bf16[768]{0:T(1024)(128)(2,1)S(1)}, f32[1024,768]{1,0:T(8,128)}) fusion(bf16[768,2304]{1,0:T(8,128)(2,1)S(1)} %bitcast.101, bf16[1024,768]{1,0:T(8,128)(2,1)S(1)} %get-tuple-element.23, bf16[1024,768]{1,0:T(8,128)(2,1)S(1)} %get-tuple-element.22, bf16[1024,768]{1,0:T(8,128)(2,1)S(1)} %get-tuple-element.21), kind=kOutput, calls=%fused_computation.109 | convolution fusion | flops 3638820096 | bytes 11404800 | tf_op jit(solution)/shard_map/dot_general | solution.py:35
  266.7 4.1 convolution_convert_fusion.4
  271.4 3.7 copy.70
  275.1 2.6 fusion.23
  280.0 3.5 fusion.24
  291.9 10.0 %convolution_convert_fusion.1 = bf16[768,3072]{1,0:T(8,128)(2,1)} fusion(bf16[1024,3072]{1,0:T(8,128)(2,1)} %copy-done.26, f32[1024,768]{0,1:T(8,128)S(1)} %copy-done.8, f32[768]{0:T(1024)S(1)} %reshape.380, f32[768]{0:T(1024)S(1)} %reshape.379, f32[1024]{0:T(1024)S(1)} %fusion.41, f32[1024]{0:T(1024)S(1)} %broadcast_multiply_fusion), kind=kOutput, calls=%fused_computation.13 | convolution fusion | flops 4838129664 | bytes 14170112 | tf_op jit(solution)/shard_map/dot_general | solution.py:29
  301.8 9.9 %reshape.371 = bf16[32,24,4,768]{3,2,1,0:T(4,128)(2,1)} reshape(bf16[768,3072]{1,0:T(8,128)(2,1)} %convolution_convert_fusion.1) | data formatting | bytes 9437184 | tf_op jit(solution)/shard_map/reshape | solution.py:191
  311.7 3.5 copy.75
  315.2 12.0 %convolution_convert_fusion = bf16[3072,768]{1,0:T(8,128)(2,1)S(1)} fusion(bf16[1024,768]{0,1:T(8,128)(2,1)S(1)} %copy-done.15, f32[1024]{0:T(1024)S(1)} %fusion.39, f32[1024,3072]{1,0:T(8,128)} %fusion.43, f32[3072]{0:T(1024)S(1)} %reshape.381), kind=kOutput, calls=%fused_computation.12 | convolution fusion | flops 4868014080 | bytes 18890752 | tf_op jit(solution)/shard_map/dot_general | solution.py:29
  327.2 3.9 pad_maximum_fusion
  331.9 11.8 %multiply_convert_fusion.1 = bf16[1024,768]{0,1:T(8,128)(2,1)} fusion(f32[1024,768]{0,1:T(8,128)S(1)} %copy-done.8, bf16[3072,768]{1,0:T(8,128)(2,1)} %bitcast.95, f32[768]{0:T(1024)S(1)} %reshape.382, f32[1024]{0:T(1024)S(1)} %fusion.39, f32[1024,3072]{1,0:T(8,128)} %fusion.43, f32[3072]{0:T(1024)S(1)} %reshape.381), kind=kOutput, calls=%fused_computation.43 | convolution fusion | flops 4866441216 | bytes 22039552 | tf_op jit(solution)/shard_map/dot_general | solution.py:271
  343.7 2.7 copy.77
  348.8 51.0 %reduce-scatter.3.cloned.1.call-done = bf16[112,768]{1,0:T(8,128)(2,1)} async-done(((bf16[3584,768]{1,0:T(8,128)(2,1)}), bf16[112,768]{1,0:T(8,128)(2,1)}) %reduce-scatter.3.cloned.1.call-update) | async-done | bytes 172048 | tf_op jit(solution)/shard_map/reduce_scatter | solution.py:287
  405.7 135.4 %reduce-scatter.5.cloned.1.call-done = bf16[192,768]{1,0:T(8,128)(2,1)} async-done(((bf16[6144,768]{1,0:T(8,128)(2,1)}), bf16[192,768]{1,0:T(8,128)(2,1)}) %reduce-scatter.5.cloned.1.call-update) | async-done | bytes 294928 | tf_op jit(solution)/shard_map/reduce_scatter | solution.py:287
  (146 shorter events, 52.4 us)
Async XLA Ops:
  7.2 10.6 %copy-start.19 = (bf16[1024,768]{1,0:T(8,128)(2,1)S(1)}, bf16[1024,768]{1,0:T(8,128)(2,1)}, u32[]{:S(2)}) copy-start(bf16[1024,768]{1,0:T(8,128)(2,1)} %param.15) | copy-start | bytes 4718596
  7.2 72.7 %all-gather.3.cloned.1.call-start = ((), (), s32[]{:S(2)}) async-start(), calls=%async_computation.2 | async-start | bytes 4460544 | tf_op jit(solution)/shard_map/all_gather | solution.py:230
  14.5 154.6 %all-gather.5.cloned.1.call-start = ((), (), s32[]{:S(2)}) async-start(), calls=%async_computation.3 | async-start | bytes 10948608 | tf_op jit(solution)/shard_map/all_gather | solution.py:230
  17.1 382.7 %reduce-scatter.3.cloned.1.call-start = ((), (), s32[]{:S(2)}) async-start(), calls=%async_computation.4 | async-start | bytes 5677056 | tf_op jit(solution)/shard_map/reduce_scatter | solution.py:287
  18.6 162.1 %copy-start.3 = (bf16[1024,768]{0,1:T(8,128)(2,1)}, bf16[1024,768]{0,1:T(8,128)(2,1)S(1)}, u32[]{:S(2)}) copy-start(bf16[1024,768]{0,1:T(8,128)(2,1)S(1)} %copy.62) | copy-start | bytes 4718596
  93.9 1.8 copy-start.17
  119.7 2.2 copy-start
  121.9 104.0 %copy-start.1 = (bf16[1024,768]{1,0:T(8,128)(2,1)}, bf16[1024,768]{1,0:T(8,128)(2,1)S(1)}, u32[]{:S(2)}) copy-start(bf16[1024,768]{1,0:T(8,128)(2,1)S(1)} %get-tuple-element.19.out_ref) | copy-start | bytes 4718596
  170.4 10.4 %copy-start.23 = (bf16[32,24,768]{2,1,0:T(8,128)(2,1)}, bf16[32,24,768]{2,1,0:T(8,128)(2,1)S(1)}, u32[]{:S(2)}) copy-start(bf16[32,24,768]{2,1,0:T(8,128)(2,1)S(1)} %slice.118) | copy-start | bytes 3538948
  182.4 9.0 %copy-start.6 = (f32[1024,768]{0,1:T(8,128)}, f32[1024,768]{0,1:T(8,128)S(1)}, u32[]{:S(2)}) copy-start(f32[1024,768]{0,1:T(8,128)S(1)} %get-tuple-element.95) | copy-start | bytes 9437188
  182.4 8.9 %slice-start.2 = ((s8[4718592]{0:T(1024)(128)(4,1)}), s8[4194304]{0:T(1024)(128)(4,1)S(1)}, s32[]{:S(2)}) async-start(s8[4718592]{0:T(1024)(128)(4,1)} %bitcast.96), calls=%async_computation.8 | async-start | bytes 8388608
  182.8 8.5 %copy-start.13 = (bf16[1024,768]{0,1:T(8,128)(2,1)S(1)}, bf16[1024,768]{0,1:T(8,128)(2,1)}, u32[]{:S(2)}) copy-start(bf16[1024,768]{0,1:T(8,128)(2,1)} %copy.68) | copy-start | bytes 4718596
  182.9 8.5 %slice-start.3 = ((s8[4718592]{0:T(1024)(128)(4,1)}), s8[524288]{0:T(1024)(128)(4,1)S(1)}, s32[]{:S(2)}) async-start(s8[4718592]{0:T(1024)(128)(4,1)} %bitcast.96), calls=%async_computation.9 | async-start | bytes 1048576
  206.4 6.8 %copy-start.26 = (bf16[1024,3072]{1,0:T(8,128)(2,1)}, bf16[1024,3072]{1,0:T(8,128)(2,1)S(1)}, u32[]{:S(2)}) copy-start(bf16[1024,3072]{1,0:T(8,128)(2,1)S(1)} %get-tuple-element.101) | copy-start | bytes 18874372
  216.8 3.9 copy-start.7
  216.8 4.7 copy-start.10
  222.3 1.7 copy-start.11
  222.3 2.2 copy-start.24
  222.3 6.1 %slice-start = ((s8[4718592]{0:T(1024)(128)(4,1)}), s8[4194304]{0:T(1024)(128)(4,1)S(1)}, s32[]{:S(2)}) async-start(s8[4718592]{0:T(1024)(128)(4,1)} %bitcast.83), calls=%async_computation.6 | async-start | bytes 8388608
  224.5 3.9 slice-start.1
  229.9 25.4 %copy-start.4 = (bf16[1024,768]{0,1:T(8,128)(2,1)S(1)}, bf16[1024,768]{0,1:T(8,128)(2,1)}, u32[]{:S(2)}) copy-start(bf16[1024,768]{0,1:T(8,128)(2,1)} %copy-done.3) | copy-start | bytes 4718596
  257.9 2.6 copy-start.18
  271.4 3.7 copy-start.5
  275.1 2.8 copy-start.9
  277.7 2.0 copy-start.12
  277.7 2.4 copy-start.14
  280.0 3.8 copy-start.22
  283.9 4.7 copy-start.20
  289.7 2.2 copy-start.8
  290.7 250.3 %reduce-scatter.5.cloned.1.call-start = ((), (), s32[]{:S(2)}) async-start(), calls=%async_computation.5 | async-start | bytes 9732096 | tf_op jit(solution)/shard_map/reduce_scatter | solution.py:287
  311.7 3.5 copy-start.15
  343.7 2.7 copy-start.16
  (3 other events, 3.7 us)
Sparse Core Ops, SparseCore 0:
  14.6 65.2 all-gather.2
  83.3 85.6 all-gather.4
  290.8 108.9 reduce-scatter.2
  406.6 134.4 reduce-scatter.4

commit v2 on v1

--- a/solution.py
+++ b/solution.py
@@ -184,16 +184,6 @@
     )
 
 
-def fold_all(full, parts, width):
-    rows = full.shape[0] // parts
-    count = full.shape[1] // width
-    return (
-        full.reshape(parts, rows, count, width)
-        .transpose(0, 2, 1, 3)
-        .reshape(parts, count * rows, width)
-    )
-
-
 def unfold_one(stacked, count):
     return unfold(stacked[None], count)
 
@@ -278,20 +268,26 @@
     grad_act = back_product(grad_out_low, down_weight)
     gelu_back = jax.vjp(gelu_tanh, hidden_pre)[1]
     grad_hidden = gelu_back(grad_act)[0].astype(jnp.bfloat16)
-    grad_w_up = weight_grad(normed_two, grad_hidden).astype(jnp.bfloat16)
+    grad_w_up = [
+        weight_grad(
+            normed_two, grad_hidden[:, index * model_width : (index + 1) * model_width]
+        ).astype(jnp.bfloat16)
+        for index in range(up_count)
+    ]
     grad_b_up = jnp.sum(grad_hidden.astype(jnp.float32), axis=0)
 
-    def scattered(pieces):
-        stacked = jnp.concatenate(pieces, axis=1)
-        flat = stacked.reshape(-1, model_width)
+    def packed(pieces):
+        return jnp.concatenate(pieces, axis=1).reshape(-1, model_width)
+
+    def scattered(flat):
         return lax.psum_scatter(flat, "fsdp", scatter_dimension=0, tiled=True)
 
-    mlp_shard = scattered(
-        [
-            fold_all(grad_w_up, parts, model_width),
-            grad_w_down.reshape(parts, -1, model_width),
-        ]
-    ).astype(jnp.float32)
+    mlp_packed = packed(
+        [part.reshape(parts, -1, model_width) for part in grad_w_up]
+        + [grad_w_down.reshape(parts, -1, model_width)]
+    )
+    mlp_packed, grad_hidden = lax.optimization_barrier((mlp_packed, grad_hidden))
+    mlp_shard = scattered(mlp_packed).astype(jnp.float32)
 
     grad_middle_norm, grad_ln2_gain, grad_ln2_bias = norm_two_back(
         back_product(grad_hidden, up_weight)
@@ -330,10 +326,11 @@
         vector_rows_grad,
         ((0, 0), (0, vector_rows - 1), (0, model_width - vector_rows_grad.shape[2])),
     )
-    attn_shard = scattered(
+    attn_packed = packed(
         [part.reshape(parts, -1, model_width) for part in grad_w_qkv]
         + [grad_w_out.reshape(parts, -1, model_width), padded]
-    ).astype(jnp.float32)
+    )
+    attn_shard = scattered(attn_packed).astype(jnp.float32)
     grad_vector_shards = []
     offset = 0
     for vector in vectors:

time: 559 us -> 587 us (1.050)
  waiting for transfers between devices: 291 us -> 331 us
  local copies, waits for them, and re-layouts: 84.6 us -> 78.7 us
    reduce_scatter x2, waiting for transfers between devices: 186 us -> 226 us  [scattered(): return lax.psum_scatter(flat, 'fsdp', scatter_dimension=0, tiled=True)]
    reshape x2 -> x0, local copies, waits for them, and re-layouts: 13.4 us -> none  [fold_all(): full.reshape(parts, rows, count, width).transpose(0, 2, 1, 3)]
    unnamed x75 -> x85, local copies, waits for them, and re-layouts: 28.7 us -> 33.7 us
    dot_general x6 -> x9, matrix products: 33.7 us -> 29.8 us  [weight_grad(): lax.dot_general(left, right, (((0,), (0,)), ((), ())), preferred_element_...]
  transfers between devices with their start and end apart: 4 -> 4, of which waited for: 4 -> 4; matrix products, arithmetic and copies ran while one was open for 16% -> 8% of each run, Pallas kernels for 4% -> 3%
where the time goes in v2:
time: 587 us; the launch traced here: 578 us
  waiting for transfers between devices  331 us (56%)
  matrix products  86.2 us (15%)
  local copies, waits for them, and re-layouts  78.7 us (13%)
  Pallas kernels  44.8 us (8%)
  other arithmetic  22.2 us (4%)
  between operations  15.5 us (3%)
    reduce_scatter x2, waiting for transfers between devices, scattered(): return lax.psum_scatter(flat, 'fsdp', scatter_dimension=0, tiled=True)  226 us
    all_gather x2, waiting for transfers between devices, gathered(): whole = lax.all_gather(stacked, 'fsdp', axis=0, tiled=True)  104 us
    unnamed x85, local copies, waits for them, and re-layouts  33.7 us
    dot_general x4, matrix products, back_product(): lax.dot_general(grad_low, weight, (((1,), (1,)), ((), ())), preferred_ele...  32.7 us
    dot_general x9, matrix products, weight_grad(): lax.dot_general(left, right, (((0,), (0,)), ((), ())), preferred_element_...  29.8 us
    pallas_call x1, Pallas kernels, attend_back(): pl.pallas_call(functools.partial(attend_back_kernel, block), grid=(pairs,...  25.5 us
    pallas_call x1, Pallas kernels, attend(): pl.pallas_call(functools.partial(attend_kernel, block), grid=(pairs,), in...  19.4 us
    dot_general x1, matrix products, local(): jnp.dot(activated, down_weight, preferred_element_type=jnp.float32)  12.3 us
  transfers between devices with their start and end apart: 4, of which 4 were waited for; matrix products, arithmetic and copies ran while one was open for 8% of the time, Pallas kernels for 3%

profile of v2, /device:TPU:0, one launch (start us, length us, event | category | flops | bytes accessed | tf_op | source)
XLA Modules:
  0.0 578.3 jit_solution(15425638289496684104)
XLA Ops:
  7.2 5.5 concatenate.57
  18.6 3.2 copy.67
  22.5 57.3 %all-gather.3.cloned.1.call-done = bf16[2816,768]{1,0:T(8,128)(2,1)} async-done(((bf16[88,768]{1,0:T(8,128)(2,1)}), bf16[2816,768]{1,0:T(8,128)(2,1)}) %all-gather.3.cloned.1.call-update) | async-done | bytes 4325392 | tf_op jit(solution)/shard_map/all_gather | solution.py:220
  79.8 4.0 slice.130
  88.6 4.5 copy.63
  95.6 4.6 add_convert_fusion.q_ref.k_ref.v_ref
  100.2 19.4 %shard_map.254 = (bf16[1024,768]{1,0:T(8,128)(2,1)S(1)}, f32[6,8,1024]{2,1,0:T(8,128)S(1)}) custom-call(bf16[1024,2304]{1,0:T(8,128)(2,1)S(1)} %add_convert_fusion.q_ref.k_ref.v_ref, bf16[1024,2304]{1,0:T(8,128)(2,1)S(1)} %add_convert_fusion.q_ref.k_ref.v_ref, bf16[1024,2304]{1,0:T(8,128)(2,1)S(1)} %add_convert_fusion.q_ref.k_ref.v_ref), custom_call_target="tpu_custom_call" | custom-call | flops 3221225472 | bytes 6291456 | tf_op jit(solution)/shard_map/pallas_call | solution.py:137
  121.8 47.1 %all-gather.5.cloned.1.call-done = bf16[6912,768]{1,0:T(8,128)(2,1)} async-done(((bf16[216,768]{1,0:T(8,128)(2,1)}), bf16[6912,768]{1,0:T(8,128)(2,1)}) %all-gather.5.cloned.1.call-update) | async-done | bytes 10616848 | tf_op jit(solution)/shard_map/all_gather | solution.py:220
  170.2 7.0 %fusion.70 = (bf16[32,96,768]{2,1,0:T(8,128)(2,1)S(1)}, bf16[32,96,768]{2,1,0:T(8,128)(2,1)}) fusion(bf16[32,216,768]{2,1,0:T(8,128)(2,1)} %bitcast.97), kind=kLoop, calls=%fused_computation.120 | loop fusion | bytes 18874368 | tf_op jit(solution)/shard_map/slice | solution.py:239
  184.0 5.3 fusion.76
  189.3 10.9 %convolution_convert_fusion = bf16[3072,768]{1,0:T(8,128)(2,1)} fusion(bf16[1024,768]{0,1:T(8,128)(2,1)S(1)} %copy-done.14, f32[1024]{0:T(1024)S(1)} %fusion.59, f32[1024,3072]{1,0:T(8,128)S(1)} %fusion.76, f32[3072]{0:T(1024)S(1)} %reshape.389), kind=kOutput, calls=%fused_computation.11 | convolution fusion | flops 4868014080 | bytes 18890752 | tf_op jit(solution)/shard_map/dot_general | solution.py:29
  200.2 15.9 %fusion.75 = (bf16[3072]{0:T(1024)(128)(2,1)S(1)}, bf16[1024,3072]{1,0:T(8,128)(2,1)}) fusion(f32[1024,3072]{1,0:T(8,128)S(1)} %fusion.76, f32[3072]{0:T(1024)S(1)} %reshape.389, bf16[3072,768]{1,0:T(8,128)(2,1)} %bitcast.101, bf16[1024,768]{0,1:T(8,128)(2,1)S(1)} %copy-done.14, f32[1024]{0:T(1024)S(1)} %fusion.59), kind=kOutput, calls=%fused_computation.125 | convolution fusion | flops 4903400448 | bytes 25188352 | tf_op jit(solution)/shard_map/dot_general | solution.py:35
  216.1 3.0 fusion.44
  228.2 2.4 constant_dynamic-update-slice_fusion
  230.6 9.7 %fusion.74 = (bf16[768]{0:T(1024)(128)(2,1)S(1)}, f32[1024,768]{1,0:T(8,128)}) fusion(bf16[1024,3072]{1,0:T(8,128)(2,1)} %get-tuple-element.22, bf16[768,3072]{1,0:T(8,128)(2,1)} %bitcast.92), kind=kOutput, calls=%fused_computation.124 | convolution fusion | flops 4832623616 | bytes 14157312 | tf_op jit(solution)/shard_map/dot_general | solution.py:35
  240.4 3.7 copy.68
  244.1 3.9 multiply_reduce_fusion
  253.2 2.5 convolution_convert_fusion.2
  257.1 25.5 %shard_map.255 = (bf16[1024,768]{1,0:T(8,128)(2,1)S(1)}, bf16[1024,768]{1,0:T(8,128)(2,1)S(1)}, bf16[1024,768]{1,0:T(8,128)(2,1)S(1)}) custom-call(bf16[1024,2304]{1,0:T(8,128)(2,1)S(1)} %bitcast.89, bf16[1024,2304]{1,0:T(8,128)(2,1)S(1)} %bitcast.89, bf16[1024,2304]{1,0:T(8,128)(2,1)S(1)} %bitcast.89, bf16[1024,768]{1,0:T(8,128)(2,1)S(1)} %copy-done.2, ...), custom_call_target="tpu_custom_call" | custom-call | flops 8053063680 | bytes 12582912 | tf_op jit(solution)/shard_map/pallas_call | solution.py:157
  282.6 2.6 convolution_convert_fusion.4
  285.2 2.6 convolution_convert_fusion.5
  287.8 5.6 fusion.73
  294.0 4.0 convolution_convert_fusion.3
  298.7 3.6 copy.69
  302.3 2.6 fusion.23
  307.3 3.3 fusion.24
  313.3 2.4 constant_dynamic-update-slice_fusion.6
  319.8 12.3 %multiply_convert_fusion.1 = bf16[1024,768]{0,1:T(8,128)(2,1)} fusion(f32[1024,768]{0,1:T(8,128)S(1)} %copy-done.8, bf16[3072,768]{1,0:T(8,128)(2,1)} %bitcast.102, f32[768]{0:T(1024)S(1)} %reshape.390, f32[1024]{0:T(1024)S(1)} %fusion.59, f32[1024,3072]{1,0:T(8,128)} %copy-done.16, f32[3072]{0:T(1024)S(1)} %reshape.389), kind=kOutput, calls=%fused_computation.41 | convolution fusion | flops 4866441216 | bytes 22039552 | tf_op jit(solution)/shard_map/dot_general | solution.py:261
  332.1 2.8 copy.75
  334.8 2.4 copy.76
  337.2 89.8 %reduce-scatter.3.cloned.1.call-done = bf16[112,768]{1,0:T(8,128)(2,1)} async-done(((bf16[3584,768]{1,0:T(8,128)(2,1)}), bf16[112,768]{1,0:T(8,128)(2,1)}) %reduce-scatter.3.cloned.1.call-update) | async-done | bytes 172048 | tf_op jit(solution)/shard_map/reduce_scatter | solution.py:283
  432.8 135.8 %reduce-scatter.5.cloned.1.call-done = bf16[192,768]{1,0:T(8,128)(2,1)} async-done(((bf16[6144,768]{1,0:T(8,128)(2,1)}), bf16[192,768]{1,0:T(8,128)(2,1)}) %reduce-scatter.5.cloned.1.call-update) | async-done | bytes 294928 | tf_op jit(solution)/shard_map/reduce_scatter | solution.py:283
  (158 shorter events, 57.7 us)
Async XLA Ops:
  7.2 10.6 %copy-start.20 = (bf16[1024,768]{1,0:T(8,128)(2,1)S(1)}, bf16[1024,768]{1,0:T(8,128)(2,1)}, u32[]{:S(2)}) copy-start(bf16[1024,768]{1,0:T(8,128)(2,1)} %param.15) | copy-start | bytes 4718596
  7.2 72.7 %all-gather.3.cloned.1.call-start = ((), (), s32[]{:S(2)}) async-start(), calls=%async_computation.2 | async-start | bytes 4460544 | tf_op jit(solution)/shard_map/all_gather | solution.py:220
  14.5 154.4 %all-gather.5.cloned.1.call-start = ((), (), s32[]{:S(2)}) async-start(), calls=%async_computation.3 | async-start | bytes 10948608 | tf_op jit(solution)/shard_map/all_gather | solution.py:220
  17.1 409.8 %reduce-scatter.3.cloned.1.call-start = ((), (), s32[]{:S(2)}) async-start(), calls=%async_computation.4 | async-start | bytes 5677056 | tf_op jit(solution)/shard_map/reduce_scatter | solution.py:283
  18.6 162.0 %copy-start.3 = (bf16[1024,768]{0,1:T(8,128)(2,1)}, bf16[1024,768]{0,1:T(8,128)(2,1)S(1)}, u32[]{:S(2)}) copy-start(bf16[1024,768]{0,1:T(8,128)(2,1)S(1)} %copy.61) | copy-start | bytes 4718596
  22.5 61.3 %copy-start.27 = (f32[1024]{0:T(1024)}, f32[1024]{0:T(1024)S(1)}, u32[]{:S(2)}) copy-start(f32[1024]{0:T(1024)S(1)} %fusion.22) | copy-start | bytes 12292
  119.6 2.2 copy-start
  121.8 131.5 %copy-start.1 = (bf16[1024,768]{1,0:T(8,128)(2,1)}, bf16[1024,768]{1,0:T(8,128)(2,1)S(1)}, u32[]{:S(2)}) copy-start(bf16[1024,768]{1,0:T(8,128)(2,1)S(1)} %get-tuple-element.21.out_ref) | copy-start | bytes 4718596
  170.2 10.4 %copy-start.24 = (bf16[32,24,768]{2,1,0:T(8,128)(2,1)}, bf16[32,24,768]{2,1,0:T(8,128)(2,1)S(1)}, u32[]{:S(2)}) copy-start(bf16[32,24,768]{2,1,0:T(8,128)(2,1)S(1)} %slice.134) | copy-start | bytes 3538948
  180.6 3.4 copy-start.13
  184.0 5.3 copy-start.14
  189.3 11.0 %copy-start.16 = (f32[1024,3072]{1,0:T(8,128)}, f32[1024,3072]{1,0:T(8,128)S(1)}, u32[]{:S(2)}) copy-start(f32[1024,3072]{1,0:T(8,128)S(1)} %fusion.76) | copy-start | bytes 37748740
  216.1 3.3 copy-start.29
  220.8 7.4 %slice-start.2 = ((s8[4718592]{0:T(1024)(128)(4,1)}), s8[4194304]{0:T(1024)(128)(4,1)S(1)}, s32[]{:S(2)}) async-start(s8[4718592]{0:T(1024)(128)(4,1)} %bitcast.98), calls=%async_computation.8 | async-start | bytes 8388608
  222.2 6.0 %slice-start.3 = ((s8[4718592]{0:T(1024)(128)(4,1)}), s8[524288]{0:T(1024)(128)(4,1)S(1)}, s32[]{:S(2)}) async-start(s8[4718592]{0:T(1024)(128)(4,1)} %bitcast.98), calls=%async_computation.9 | async-start | bytes 1048576
  244.1 3.9 copy-start.7
  244.1 4.7 copy-start.10
  249.6 2.2 copy-start.25
  249.6 6.1 %slice-start = ((s8[4718592]{0:T(1024)(128)(4,1)}), s8[4194304]{0:T(1024)(128)(4,1)S(1)}, s32[]{:S(2)}) async-start(s8[4718592]{0:T(1024)(128)(4,1)} %bitcast.88), calls=%async_computation.6 | async-start | bytes 8388608
  251.8 3.9 slice-start.1
  257.1 25.5 %copy-start.4 = (bf16[1024,768]{0,1:T(8,128)(2,1)S(1)}, bf16[1024,768]{0,1:T(8,128)(2,1)}, u32[]{:S(2)}) copy-start(bf16[1024,768]{0,1:T(8,128)(2,1)} %copy-done.3) | copy-start | bytes 4718596
  285.2 2.6 copy-start.19
  298.7 3.6 copy-start.5
  302.3 2.6 copy-start.28
  302.3 2.8 copy-start.9
  304.9 2.0 copy-start.12
  304.9 2.4 copy-start.15
  307.3 3.7 copy-start.23
  311.0 4.7 copy-start.21
  317.9 1.9 copy-start.8
  317.9 250.8 %reduce-scatter.5.cloned.1.call-start = ((), (), s32[]{:S(2)}) async-start(), calls=%async_computation.5 | async-start | bytes 9732096 | tf_op jit(solution)/shard_map/reduce_scatter | solution.py:283
  332.1 2.8 copy-start.17
  (6 other events, 8.7 us)
Sparse Core Ops, SparseCore 0:
  14.6 65.2 all-gather.2
  83.3 85.5 all-gather.4
  318.0 108.8 reduce-scatter.2
  433.7 134.9 reduce-scatter.4
